TPU v7x, 512 devices: a whole 4x4x16 slice. The times are simulated.
512 devices in a mesh: pair: 8 (over z_hi, y), blk: 64 (over z_lo, x, core).
Axes of the slice: x: 4, y: 4, z: 16 (z_hi: 2, z_lo: 8; z = z_hi * 8 + z_lo), core: 2. Of those that a mesh axis runs over, the one named last changes fastest.
Arguments:
- amps: bfloat16 [8192, 80200], P(('blk', 'pair')), may hold values from -6 to 6
- ints: bfloat16 [1024, 80200], P('blk', 'pair'), may hold values from -0.015625 to 0.015625
- block_of: int32 [64], replicated, may hold values from 0 to 63, each once
- pair_rows: int32 [8192, 2], P(('blk', 'pair')), may hold values from 0 to 119
- occ_energy: float32 [120], replicated, may hold values from -2 to -0.5
- vir_pair_energy: float32 [1024], replicated, may hold values from 1 to 6
Outputs:
- new_amps: float32 [8192, 1024], P(('blk', 'pair'))
Inputs may be any that keep to these rules, and one draw needn't show every extreme that they name: `block_of`: each of 0 to 63 once.
All inputs are finite; a program needn't handle non-finite values.
Results may differ from a plain program's by a relative error of at most 0.0003.
Values may be sent and summed in bfloat16 or wider, within the bound.
A program may use at most 128 MiB of HBM per device.

v0:
```python
import jax
import jax.numpy as jnp
from jax import lax
from jax.sharding import PartitionSpec as P

NV = 400


def contract(weighted, slab_part):
    return lax.dot_general(
        weighted, slab_part, (((1,), (1,)), ((), ())), preferred_element_type=jnp.float32
    )


def per_device(amps, ints, block_of, pair_rows, occ_energy, vir_pair_energy):
    relaid = lax.all_to_all(amps, "pair", split_axis=1, concat_axis=0, tiled=True)
    shard_width = relaid.shape[1]
    column = lax.axis_index("pair") * shard_width + lax.broadcasted_iota(
        jnp.int32, (1, shard_width), 1
    )
    weighted = relaid * jnp.where(column < NV, 1.0, 2.0).astype(jnp.bfloat16)
    gathered = lax.all_gather(ints, "blk", axis=0, tiled=True)
    stored = contract(weighted, gathered)
    summed = lax.psum_scatter(stored, "pair", scatter_dimension=0, tiled=True)
    blocks = block_of.shape[0]
    height = summed.shape[0]
    grouped = summed.reshape(height, blocks, summed.shape[1] // blocks)
    ladder = jnp.zeros_like(grouped).at[:, block_of].set(grouped).reshape(height, summed.shape[1])
    levels = lax.broadcasted_iota(jnp.int32, (1, 1, occ_energy.shape[0]), 2)
    one_hot = (pair_rows[:, :, None] == levels).astype(jnp.float32)
    occupied = jnp.sum(one_hot * occ_energy[None, None, :], axis=(1, 2))
    denominator = vir_pair_energy[None, :] - occupied[:, None]
    return ladder / denominator


def solution(mesh):
    placed = (P(("blk", "pair"), None), P("blk", "pair"), P(), P(("blk", "pair"), None), P(), P())
    return jax.shard_map(
        per_device, mesh=mesh, in_specs=placed, out_specs=P(("blk", "pair"), None), check_vma=False
    )
```

profile of v0, /device:TPU:1, one launch (start us, length us, event | category | flops | bytes accessed | tf_op | source)
XLA Modules:
  0.0 403.0 jit_solution(10764181286795484275)
XLA Ops:
  6.5 0.0 all-gather.2.cloned.1.call-start
  6.5 0.7 all-gather.2.cloned.1.call-update
  7.3 4.8 %all_to_all.14 = bf16[16,8,10025]{2,1,0:T(8,128)(2,1)S(1)} reshape(bf16[16,80200]{1,0:T(8,128)(2,1)} %param.6) | data formatting | bytes 5132800 | tf_op jit(solution)/shard_map/all_to_all | solution.py:16
  12.1 1.8 copy.13
  13.9 18.3 %all-to-all-start = ((bf16[16,8,10025]{2,0,1:T(8,128)(2,1)}), bf16[16,8,10025]{2,0,1:T(8,128)(2,1)}, u32[]{:S(2)}, u32[]{:S(2)}) async-start(bf16[16,8,10025]{2,0,1:T(8,128)(2,1)} %copy.13), calls=%async_computation | async-start | bytes 5177344 | tf_op jit(solution)/shard_map/all_to_all | solution.py:16
  32.1 0.0 reduce-scatter.2.cloned.1.call-start
  32.2 144.2 %all-to-all-done = bf16[16,8,10025]{2,0,1:T(8,128)(2,1)} async-done(((bf16[16,8,10025]{2,0,1:T(8,128)(2,1)}), bf16[16,8,10025]{2,0,1:T(8,128)(2,1)}, u32[]{:S(2)}, u32[]{:S(2)}) %all-to-all-start) | async-done | bytes 2566432 | tf_op jit(solution)/shard_map/all_to_all | solution.py:16
  176.4 2.1 bitcast_multiply_fusion
  178.6 0.0 copy-start.1
  178.6 0.0 copy-start.2
  178.6 0.0 copy-start.3
  178.6 90.1 %all-gather.2.cloned.1.call-done = bf16[1024,10025]{1,0:T(8,128)(2,1)} async-done(((bf16[16,10025]{1,0:T(8,128)(2,1)}), bf16[1024,10025]{1,0:T(8,128)(2,1)}) %all-gather.2.cloned.1.call-update) | async-done | bytes 20531216 | tf_op jit(solution)/shard_map/all_gather | solution.py:22
  268.7 11.9 %fusion = f32[128,1024]{1,0:T(8,128)} fusion(bf16[128,10025]{1,0:T(8,128)(2,1)S(1)} %bitcast_multiply_fusion, bf16[1024,10025]{1,0:T(8,128)(2,1)} %all-gather.2.cloned.1.call-done), kind=kOutput, calls=%fused_computation.8 | convolution fusion | flops 2627993600 | bytes 23621888 | tf_op jit(solution)/shard_map/dot_general | solution.py:10
  280.6 0.0 reduce-scatter.2.cloned.1.call-update
  280.6 0.0 copy-done.1
  280.6 0.0 copy-done.2
  280.6 0.2 select_reduce_fusion
  280.8 0.0 copy-done.3
  280.8 0.0 copy-start
  280.8 110.3 %reduce-scatter.2.cloned.1.call-done = f32[16,1024]{1,0:T(8,128)} async-done(((f32[128,1024]{1,0:T(8,128)}), f32[16,1024]{1,0:T(8,128)}) %reduce-scatter.2.cloned.1.call-update) | async-done | bytes 65552 | tf_op jit(solution)/shard_map/reduce_scatter | solution.py:24
  391.2 1.0 reshape.27
  392.2 0.3 copy.14
  392.6 2.4 scatter_fusion
  395.0 0.2 copy.15
  395.2 0.3 reshape.25
  395.5 0.0 copy-done
  395.5 0.7 subtract_divide_fusion
  (3 shorter events, 0.1 us)
Async XLA Ops:
  6.5 262.2 %all-gather.2.cloned.1.call-start = ((), (), s32[]{:S(2)}) async-start(), calls=%async_computation.2 | async-start | bytes 21032960 | tf_op jit(solution)/shard_map/all_gather | solution.py:22
  13.9 162.6 %all-to-all-start = ((bf16[16,8,10025]{2,0,1:T(8,128)(2,1)}), bf16[16,8,10025]{2,0,1:T(8,128)(2,1)}, u32[]{:S(2)}, u32[]{:S(2)}) async-start(bf16[16,8,10025]{2,0,1:T(8,128)(2,1)} %copy.13), calls=%async_computation | async-start | bytes 5177344 | tf_op jit(solution)/shard_map/all_to_all | solution.py:16
  32.1 359.0 %reduce-scatter.2.cloned.1.call-start = ((), (), s32[]{:S(2)}) async-start(), calls=%async_computation.3 | async-start | bytes 589824 | tf_op jit(solution)/shard_map/reduce_scatter | solution.py:24
  178.6 102.0 %copy-start.1 = (s32[16,2]{0,1:T(2,128)S(1)}, s32[16,2]{0,1:T(2,128)}, u32[]{:S(2)}) copy-start(s32[16,2]{0,1:T(2,128)} %param.9) | copy-start | bytes 388
  178.6 102.0 %copy-start.2 = (f32[120]{0:T(128)S(1)}, f32[120]{0:T(128)}, u32[]{:S(2)}) copy-start(f32[120]{0:T(128)} %param.10) | copy-start | bytes 1444
  178.6 102.2 %copy-start.3 = (s32[64]{0:T(128)S(1)}, s32[64]{0:T(128)}, u32[]{:S(2)}) copy-start(s32[64]{0:T(128)} %param.8) | copy-start | bytes 772
  280.8 114.6 %copy-start = (f32[1024]{0:T(1024)S(1)}, f32[1024]{0:T(1024)}, u32[]{:S(2)}) copy-start(f32[1024]{0:T(1024)} %param.11) | copy-start | bytes 12292
Sparse Core Ops, SparseCore 0:
  9.5 259.1 all-gather.1
  280.7 110.3 reduce-scatter.1
where the time goes:
time: 404 us; the launch traced here: 403 us
  waiting for transfers between devices  345 us (85%)
  starting transfers between devices  18.3 us (5%)
  between operations  13.5 us (3%)
  matrix products  11.9 us (3%)
  local copies, waits for them, and re-layouts  10.9 us (3%)
    all_to_all x1, waiting for transfers between devices, per_device(): lax.all_to_all(amps, 'pair', split_axis=1, concat_axis=0, tiled=True)  144 us
    reduce_scatter x1, waiting for transfers between devices, per_device(): summed = lax.psum_scatter(stored, 'pair', scatter_dimension=0, tiled=True)  110 us
    all_gather x1, waiting for transfers between devices, per_device(): gathered = lax.all_gather(ints, 'blk', axis=0, tiled=True)  90.1 us
    all_to_all x1, starting transfers between devices, per_device(): lax.all_to_all(amps, 'pair', split_axis=1, concat_axis=0, tiled=True)  18.3 us
    dot_general x1, matrix products, contract(): lax.dot_general(weighted, slab_part, (((1,), (1,)), ((), ())), preferred_...  11.9 us
  transfers between devices with their start and end apart: 3, of which 3 were waited for; matrix products, arithmetic and copies ran while one was open for 1% of the time, Pallas kernels for 0%

commit v1 on v0

v1 whole, which is shorter than its diff:
```python
import functools

import jax
import jax.numpy as jnp
from jax import lax
from jax.experimental import pallas as pl
from jax.experimental.pallas import tpu as pltpu
from jax.sharding import PartitionSpec as P

NV = 400
CD = 80200
RANGE = 10025
LANES = 128
WIDE = 10240
PIECE = 1280
LAST_TILE = 547
TAIL = LAST_TILE * LANES + WIDE - PIECE
Z, ZLO, Y, X = 16, 8, 4, 4
PLANE = 32
ROWS = 16
MESH = pl.DeviceIdType.MESH
F32, BF16 = jnp.float32, jnp.bfloat16

ORDER = (4, 3, 5, 2, 6, 1, 7, 0)
GROUPS = ((0, 1), (1, 3), (3, 5), (5, 7), (7, 8))
NT = (((1,), (1,)), ((), ()))


def first_tile(p):
    return jnp.minimum((RANGE * p) // LANES, LAST_TILE)


def kernel(
    amps, tail, wide, block_of, rows, occ, vir, out,
    a_buf, g_buf, prep, part, sib, got, acc, den_buf,
    i_send, i_recv, i_own, a_send, a_recv, a_own, r_send, r_recv, s_send, s_recv, q_send, q_recv,
):
    pair, blk = lax.axis_index("pair"), lax.axis_index("blk")
    zh, y = pair // Y, pair % Y
    zl, x, c = blk // (X * 2), (blk // 2) % X, blk % 2
    z = zh * ZLO + zl

    def device(z_at, y_at, x_at, c_at):
        return ((z_at // ZLO) * Y + y_at, ((z_at % ZLO) * X + x_at) * 2 + c_at)

    up, down = device((z + 1) % Z, y, x, c), device((z + Z - 1) % Z, y, x, c)
    twin = device(z, y, x, 1 - c)

    def peer(k):
        dc, dy, dx = k // 16, (k // 4) % 4, k % 4
        return (y + dy) % Y, (x + dx) % X, (c + dc) % 2

    def back(k):
        dc, dy, dx = k // 16, (k // 4) % 4, k % 4
        return (y + Y - dy) % Y, (x + X - dx) % X, (c + dc) % 2

    barrier = pltpu.get_barrier_semaphore()

    def greet(k, carry):
        pl.semaphore_signal(barrier, inc=1, device_id=device(z, *peer(k)), device_id_type=MESH)
        return carry

    lax.fori_loop(1, PLANE, greet, 0)
    for where in (up, down):
        pl.semaphore_signal(barrier, inc=1, device_id=where, device_id_type=MESH)

    offset = RANGE * pair - first_tile(pair) * LANES
    shift, skip = offset % LANES, offset // LANES
    lane = lax.broadcasted_iota(jnp.int32, (ROWS, LANES), 1)
    keep = lane >= shift

    def align(i, before):
        for j in range(8):
            tile = i * 8 + j
            at = pl.ds(pl.multiple_of(tile * LANES, LANES), LANES)
            now = pltpu.roll(wide[:, at].astype(F32), shift, 1)
            to = pl.multiple_of(((tile + skip) % 80) * LANES, LANES)
            prep[:, pl.ds(to, LANES)] = jnp.where(keep, now, before).astype(BF16)
            before = now
        return before

    lax.fori_loop(0, 10, align, jnp.zeros((ROWS, LANES), F32))

    pl.semaphore_wait(barrier, PLANE - 1 + 2)

    def ints_copy(k):
        x_to, c_to = (x + k // 2) % X, (c + k % 2) % 2
        src = prep.at[:, pl.ds(pl.multiple_of((x_to * 2 + c_to) * PIECE, LANES), PIECE)]
        return src, g_buf.at[0, x * 2 + c], device(z, y, x_to, c_to)

    src, dst, _ = ints_copy(0)
    own_ints = pltpu.make_async_copy(src, dst, i_own)
    own_ints.start()

    def send_ints(k, carry):
        src, dst, where = ints_copy(k)
        pltpu.make_async_remote_copy(src, dst, i_send, i_recv, device_id=where, device_id_type=MESH).start()
        return carry

    lax.fori_loop(1, 8, send_ints, 0)

    def amps_at(half, y_to, x_to, c_to):
        q = x_to * 2 + c_to
        p = half * Y + y_to
        start = pl.multiple_of(first_tile(p) * LANES + q * PIECE, LANES)
        return start, jnp.logical_and(p == 7, q == 7)

    def send_amps(k, carry):
        y_to, x_to, c_to = peer(k)
        for half in range(2):
            start, last = amps_at(half, y_to, x_to, c_to)
            dst = a_buf.at[half, pl.ds(pl.multiple_of(k * ROWS, ROWS), ROWS)]

            @pl.when(jnp.logical_not(last))
            def _():
                pltpu.make_async_remote_copy(
                    amps.at[:, pl.ds(start, PIECE)], dst, a_send, a_recv,
                    device_id=device(z, y_to, x_to, c_to), device_id_type=MESH,
                ).start()

            @pl.when(last)
            def _():
                pltpu.make_async_remote_copy(
                    tail, dst, a_send, a_recv,
                    device_id=device(z, y_to, x_to, c_to), device_id_type=MESH,
                ).start()

        return carry

    lax.fori_loop(1, PLANE, send_amps, 0)
    for half in range(2):
        start, last = amps_at(half, y, x, c)
        dst = a_buf.at[half, 0:ROWS]

        @pl.when(jnp.logical_not(last))
        def _():
            pltpu.make_async_copy(amps.at[:, pl.ds(start, PIECE)], dst, a_own.at[half]).start()

        @pl.when(last)
        def _():
            pltpu.make_async_copy(tail, dst, a_own.at[half]).start()

    occ_lane = lax.broadcasted_iota(jnp.int32, (ROWS, occ.shape[1]), 1)
    e_i = jnp.sum(jnp.where(rows[:, 0:1] == occ_lane, occ[...], 0.0), axis=1, keepdims=True)
    e_j = jnp.sum(jnp.where(rows[:, 1:2] == occ_lane, occ[...], 0.0), axis=1, keepdims=True)
    den_buf[...] = vir[...] - (e_i + e_j)
    acc[...] = jnp.zeros_like(acc)

    own_ints.wait()
    seven = g_buf.at[0, 0:7]
    pltpu.make_async_copy(seven, seven, i_recv).wait()

    def hop(m_from, m_to, part_at, where):
        sl = pl.ds(part_at * 4, 4)
        return pltpu.make_async_remote_copy(
            g_buf.at[m_from, sl], g_buf.at[m_to, sl], r_send.at[m_to, part_at], r_recv.at[m_to, part_at],
            device_id=where, device_id_type=MESH,
        )

    def forward(step):
        for part_at in range(2):
            ways = [(step, (step - 1) % Z, up), (Z - step, (Z - step + 1) % Z, down)]
            if step == 8:
                ways = [ways[part_at]]
            for m_to, m_from, where in ways:
                if step > 1:
                    hop(m_from, m_from, part_at, where).wait_recv()
                hop(m_from, m_to, part_at, where).start()

    def compute(group):
        lo, hi = GROUPS[group]
        for o in range(lo, hi):
            b = ORDER[o]
            half = ((z + Z - b) % Z) // ZLO
            low = g_buf[b].reshape(LANES, PIECE)
            high = g_buf[b + 8].reshape(LANES, PIECE)
            part[o] = lax.dot_general(a_buf[half], low, NT, preferred_element_type=F32) + lax.dot_general(
                a_buf[1 - half], high, NT, preferred_element_type=F32
            )
        twin_copy(group).start()

    def twin_copy(group):
        lo, hi = GROUPS[group]
        return pltpu.make_async_remote_copy(
            part.at[lo:hi, 256:512], sib.at[lo:hi], s_send.at[group], s_recv.at[group],
            device_id=twin, device_id_type=MESH,
        )

    def spread(group):
        lo, hi = GROUPS[group]
        twin_copy(group).wait_recv()
        for o in range(lo, hi):
            part[o, 0:256] += sib[o]

        def send_sum(k, carry):
            sl = pl.ds(pl.multiple_of(k * ROWS, ROWS), ROWS)
            pltpu.make_async_remote_copy(
                part.at[lo:hi, sl], got.at[lo:hi, sl], q_send.at[group], q_recv.at[group],
                device_id=device(z, *back(k)), device_id_type=MESH,
            ).start()
            return carry

        lax.fori_loop(1, 16, send_sum, 0)

    def finish(group):
        lo, hi = GROUPS[group]
        arrived = got.at[lo:hi, ROWS:256]
        pltpu.make_async_copy(arrived, arrived, q_recv.at[group]).wait()
        column = lax.broadcasted_iota(jnp.int32, (1, LANES), 1)
        for o in range(lo, hi):
            total = part[o, 0:ROWS]
            for k in range(1, 16):
                total = total + got[o, k * ROWS : (k + 1) * ROWS]
            top = total.astype(BF16)
            rest = total - top.astype(F32)
            mid = rest.astype(BF16)
            low = (rest - mid.astype(F32)).astype(BF16)
            block = (zl + ZLO - ORDER[o]) % ZLO
            held = block_of[pl.ds(block, 1), :]
            goes = jnp.zeros((1, LANES), jnp.int32)
            for j in range(8):
                goes = jnp.where(column // 16 == j, held[:, j : j + 1], goes)
            goes = goes * 16 + column % 16
            place = lax.broadcasted_iota(jnp.int32, (1024, LANES), 0)
            moves = jnp.where(place == goes, 1.0, 0.0).astype(BF16)
            moved = lax.dot_general(
                jnp.concatenate([top, mid, low], axis=0), moves, NT, preferred_element_type=F32
            )
            acc[...] += moved[0:16] + moved[16:32] + moved[32:48]

    for step in range(1, 6):
        forward(step)
    pltpu.make_async_copy(amps.at[:, 0:PIECE], a_buf.at[0, 0:ROWS], a_own.at[0]).wait()
    pltpu.make_async_copy(amps.at[:, 0:PIECE], a_buf.at[1, 0:ROWS], a_own.at[1]).wait()
    others = a_buf.at[:, ROWS:512]
    pltpu.make_async_copy(others, others, a_recv).wait()
    compute(0)
    forward(6)
    spread(0)
    compute(1)
    forward(7)
    spread(1)
    compute(2)
    forward(8)
    spread(2)
    hop(7, 7, 1, up).wait_recv()
    hop(9, 9, 0, down).wait_recv()
    compute(3)
    finish(0)
    finish(1)
    spread(3)
    hop(8, 8, 0, up).wait_recv()
    hop(8, 8, 1, down).wait_recv()
    compute(4)
    finish(2)
    spread(4)
    finish(3)
    finish(4)
    out[...] = acc[...] / den_buf[...]

    pltpu.make_async_copy(seven, seven, i_send).wait()
    pltpu.make_async_copy(others, others, a_send).wait()
    for step in range(1, 9):
        for part_at in range(2):
            if step < 8 or part_at == 0:
                hop(step, step, part_at, up).wait_send()
            if step < 8 or part_at == 1:
                hop(Z - step, Z - step, part_at, down).wait_send()
    for group in range(5):
        lo, hi = GROUPS[group]
        twin_copy(group).wait_send()
        arrived = got.at[lo:hi, ROWS:256]
        pltpu.make_async_copy(arrived, arrived, q_send.at[group]).wait()


def per_device(amps, ints, block_of, pair_rows, occ_energy, vir_pair_energy):
    column = lax.axis_index("pair") * RANGE + lax.broadcasted_iota(jnp.int32, (1, RANGE), 1)
    weighted = ints * jnp.where(column < NV, 1.0, 2.0).astype(BF16)
    wide = jnp.pad(weighted, ((0, 0), (0, WIDE - RANGE)))
    tail = jnp.pad(amps[:, TAIL:], ((0, 0), (0, TAIL + PIECE - CD)))
    vmem = pl.BlockSpec(memory_space=pltpu.VMEM)
    hbm = pl.BlockSpec(memory_space=pl.ANY)
    dma = pltpu.SemaphoreType.DMA
    return pl.pallas_call(
        kernel,
        out_shape=jax.ShapeDtypeStruct((ROWS, 1024), F32),
        in_specs=[hbm, vmem, vmem, vmem, vmem, vmem, vmem],
        out_specs=vmem,
        scratch_shapes=[
            pltpu.VMEM((2, 512, PIECE), BF16),
            pltpu.VMEM((Z, 8, ROWS, PIECE), BF16),
            pltpu.VMEM((ROWS, WIDE), BF16),
            pltpu.VMEM((8, 512, LANES), F32),
            pltpu.VMEM((8, 256, LANES), F32),
            pltpu.VMEM((8, 256, LANES), F32),
            pltpu.VMEM((ROWS, 1024), F32),
            pltpu.VMEM((ROWS, 1024), F32),
            dma, dma, dma, dma, dma, dma((2,)),
            dma((Z, 2)), dma((Z, 2)), dma((5,)), dma((5,)), dma((5,)), dma((5,)),
        ],
        compiler_params=pltpu.CompilerParams(
            collective_id=0, has_side_effects=True, vmem_limit_bytes=40 * 1024 * 1024
        ),
        cost_estimate=pl.CostEstimate(flops=2700000000, bytes_accessed=4000000, transcendentals=0),
    )(
        amps, tail, wide, block_of.reshape(8, 8), pair_rows,
        occ_energy.reshape(1, -1), vir_pair_energy.reshape(1, -1),
    )


def solution(mesh):
    placed = (P(("blk", "pair"), None), P("blk", "pair"), P(), P(("blk", "pair"), None), P(), P())
    return jax.shard_map(
        per_device, mesh=mesh, in_specs=placed, out_specs=P(("blk", "pair"), None), check_vma=False
    )
```

time: 404 us -> 95.4 us (0.24)
  waiting for transfers between devices: 345 us -> 0 us
  Pallas kernels: 0 us -> 88.1 us
  starting transfers between devices: 18.3 us -> 0 us
  between operations: 13.5 us -> 0.03 us
  matrix products: 11.9 us -> 0 us
  local copies, waits for them, and re-layouts: 10.9 us -> 6.01 us
    all_to_all x1 -> x0, waiting for transfers between devices: 144 us -> none  [per_device(): lax.all_to_all(amps, 'pair', split_axis=1, concat_axis=0, tiled=True)]
    reduce_scatter x1 -> x0, waiting for transfers between devices: 110 us -> none  [per_device(): summed = lax.psum_scatter(stored, 'pair', scatter_dimension=0, tiled=True)]
    all_gather x1 -> x0, waiting for transfers between devices: 90.1 us -> none  [per_device(): gathered = lax.all_gather(ints, 'blk', axis=0, tiled=True)]
    pallas_call x0 -> x1, Pallas kernels: none -> 88.1 us  [per_device(): pl.pallas_call(kernel, out_shape=jax.ShapeDtypeStruct((ROWS, 1024), F32),...]
    all_to_all x1 -> x0, starting transfers between devices: 18.3 us -> none  [per_device(): lax.all_to_all(amps, 'pair', split_axis=1, concat_axis=0, tiled=True)]
    dot_general x1 -> x0, matrix products: 11.9 us -> none  [contract(): lax.dot_general(weighted, slab_part, (((1,), (1,)), ((), ())), preferred_...]
    all_to_all x2 -> x0, local copies, waits for them, and re-layouts: 6.61 us -> none  [per_device(): lax.all_to_all(amps, 'pair', split_axis=1, concat_axis=0, tiled=True)]
    unnamed x8, local copies, waits for them, and re-layouts: 0.03 us -> 4.46 us
  transfers between devices with their start and end apart: 3 -> 0, of which waited for: 3 -> 0; matrix products, arithmetic and copies ran while one was open for 1% -> 0% of each run, Pallas kernels for 0% -> 0%
where the time goes in v1:
time: 95.4 us; the launch traced here: 95.1 us
  Pallas kernels  88.1 us (92%)
  local copies, waits for them, and re-layouts  6.01 us (6%)
  other arithmetic  1.04 us (1%)
    pallas_call x1, Pallas kernels, per_device(): pl.pallas_call(kernel, out_shape=jax.ShapeDtypeStruct((ROWS, 1024), F32),...  88.1 us
    unnamed x8, local copies, waits for them, and re-layouts  4.46 us

profile of v1, /device:TPU:1, one launch (start us, length us, event | category | flops | bytes accessed | tf_op | source)
XLA Modules:
  0.0 95.1 jit_solution(7057036818324005247)
XLA Ops:
  0.0 1.0 %broadcast_multiply_fusion = bf16[16,10025]{1,0:T(8,128)(2,1)S(1)} fusion(bf16[16,10025]{1,0:T(8,128)(2,1)} %param.7, bf16[10025]{0:T(1024)(128)(2,1)S(1)} %select_convert_fusion), kind=kLoop, calls=%fused_computation | loop fusion | flops 160400 | bytes 661650 | tf_op jit(solution)/shard_map/mul | solution.py:278
  1.1 0.8 slice.3
  1.9 0.8 copy.7.rows
  2.6 0.7 reshape.20.block_of
  3.4 0.0 copy-start
  3.4 1.7 %copy-done = bf16[16,80200]{1,0:T(8,128)(2,1)S(1)} copy-done((bf16[16,80200]{1,0:T(8,128)(2,1)S(1)}, bf16[16,80200]{1,0:T(8,128)(2,1)}, u32[]{:S(2)}) %copy-start) | copy-done | bytes 2566424
  5.1 0.0 copy-start.1
  5.1 0.7 copy-done.1
  5.8 0.0 copy-start.2
  5.8 0.7 copy-done.2
  6.4 88.1 %shard_map.64 = f32[16,1024]{1,0:T(8,128)S(1)} custom-call(bf16[16,80200]{1,0:T(8,128)(2,1)S(1)} %copy-done, bf16[16,1280]{1,0:T(8,128)(2,1)S(1)} %pad.8.tail, bf16[16,10240]{1,0:T(8,128)(2,1)S(1)} %pad.9.wide, s32[8,8]{1,0:T(8,128)S(1)} %reshape.20.block_of, s32[16,2]{1,0:T(8,128)S(1)} %copy.7.rows, f32[1,120]{1,0:T(1,128)S(1)} %bitcast.3, ...), custom_call_target="tpu_custom_call" | custom-call | flops 2700000000 | bytes 4000000 | tf_op jit(solution)/shard_map/pallas_call | solution.py:284
  94.5 0.6 copy.9
  (3 shorter events, 0.0 us)
Async XLA Ops:
  3.4 1.7 %copy-start = (bf16[16,80200]{1,0:T(8,128)(2,1)S(1)}, bf16[16,80200]{1,0:T(8,128)(2,1)}, u32[]{:S(2)}) copy-start(bf16[16,80200]{1,0:T(8,128)(2,1)} %amps.1) | copy-start | bytes 7699204
  5.1 0.7 copy-start.1
  5.8 0.7 copy-start.2

commit v2 on v1

--- a/solution.py
+++ b/solution.py
@@ -17,6 +17,7 @@
 TAIL = LAST_TILE * LANES + WIDE - PIECE
 Z, ZLO, Y, X = 16, 8, 4, 4
 PLANE = 32
+BLOCKS = 64
 ROWS = 16
 MESH = pl.DeviceIdType.MESH
 F32, BF16 = jnp.float32, jnp.bfloat16
@@ -31,8 +32,8 @@
 
 
 def kernel(
-    amps, tail, wide, block_of, rows, occ, vir, out,
-    a_buf, g_buf, prep, part, sib, got, acc, den_buf,
+    amps, ints, block_of, rows, occ, vir, out,
+    a_buf, g_buf, held, last, tail, prep, part, sib, got, acc, den_buf, in_sem,
     i_send, i_recv, i_own, a_send, a_recv, a_own, r_send, r_recv, s_send, s_recv, q_send, q_recv,
 ):
     pair, blk = lax.axis_index("pair"), lax.axis_index("blk")
@@ -54,6 +55,11 @@
         dc, dy, dx = k // 16, (k // 4) % 4, k % 4
         return (y + Y - dy) % Y, (x + X - dx) % X, (c + dc) % 2
 
+    get_ints = pltpu.make_async_copy(ints, held, in_sem.at[0])
+    get_ints.start()
+    get_tail = pltpu.make_async_copy(amps.at[:, TAIL:CD], last.at[:, :], in_sem.at[1])
+    get_tail.start()
+
     barrier = pltpu.get_barrier_semaphore()
 
     def greet(k, carry):
@@ -69,17 +75,31 @@
     lane = lax.broadcasted_iota(jnp.int32, (ROWS, LANES), 1)
     keep = lane >= shift
 
+    def put(tile, value, before):
+        now = pltpu.roll(value, shift, 1)
+        to = pl.multiple_of(((tile + skip) % 80) * LANES, LANES)
+        prep[:, pl.ds(to, LANES)] = jnp.where(keep, now, before).astype(BF16)
+        return now
+
     def align(i, before):
-        for j in range(8):
-            tile = i * 8 + j
+        for j in range(6):
+            tile = i * 6 + j
             at = pl.ds(pl.multiple_of(tile * LANES, LANES), LANES)
-            now = pltpu.roll(wide[:, at].astype(F32), shift, 1)
-            to = pl.multiple_of(((tile + skip) % 80) * LANES, LANES)
-            prep[:, pl.ds(to, LANES)] = jnp.where(keep, now, before).astype(BF16)
-            before = now
+            column = RANGE * pair + tile * LANES + lane
+            weight = jnp.where(column < NV, 1.0, 2.0)
+            before = put(tile, held[:, at].astype(F32) * weight, before)
         return before
 
-    lax.fori_loop(0, 10, align, jnp.zeros((ROWS, LANES), F32))
+    get_ints.wait()
+    before = lax.fori_loop(0, 13, align, jnp.zeros((ROWS, LANES), F32))
+    rest = held[:, 78 * LANES : RANGE].astype(F32) * 2.0
+    rest = jnp.concatenate([rest, jnp.zeros((ROWS, 79 * LANES - RANGE), F32)], axis=1)
+    before = put(78, rest, before)
+    put(79, jnp.zeros((ROWS, LANES), F32), before)
+    get_tail.wait()
+    tail[:, 0 : PIECE - LANES] = last[:, 0 : PIECE - LANES]
+    ending = last[:, PIECE - LANES :]
+    tail[:, PIECE - LANES :] = jnp.concatenate([ending, jnp.zeros((ROWS, TAIL + PIECE - CD), BF16)], axis=1)
 
     pl.semaphore_wait(barrier, PLANE - 1 + 2)
 
@@ -108,17 +128,17 @@
     def send_amps(k, carry):
         y_to, x_to, c_to = peer(k)
         for half in range(2):
-            start, last = amps_at(half, y_to, x_to, c_to)
+            start, ends = amps_at(half, y_to, x_to, c_to)
             dst = a_buf.at[half, pl.ds(pl.multiple_of(k * ROWS, ROWS), ROWS)]
 
-            @pl.when(jnp.logical_not(last))
+            @pl.when(jnp.logical_not(ends))
             def _():
                 pltpu.make_async_remote_copy(
                     amps.at[:, pl.ds(start, PIECE)], dst, a_send, a_recv,
                     device_id=device(z, y_to, x_to, c_to), device_id_type=MESH,
                 ).start()
 
-            @pl.when(last)
+            @pl.when(ends)
             def _():
                 pltpu.make_async_remote_copy(
                     tail, dst, a_send, a_recv,
@@ -129,21 +149,27 @@
 
     lax.fori_loop(1, PLANE, send_amps, 0)
     for half in range(2):
-        start, last = amps_at(half, y, x, c)
+        start, ends = amps_at(half, y, x, c)
         dst = a_buf.at[half, 0:ROWS]
 
-        @pl.when(jnp.logical_not(last))
+        @pl.when(jnp.logical_not(ends))
         def _():
             pltpu.make_async_copy(amps.at[:, pl.ds(start, PIECE)], dst, a_own.at[half]).start()
 
-        @pl.when(last)
+        @pl.when(ends)
         def _():
             pltpu.make_async_copy(tail, dst, a_own.at[half]).start()
 
     occ_lane = lax.broadcasted_iota(jnp.int32, (ROWS, occ.shape[1]), 1)
-    e_i = jnp.sum(jnp.where(rows[:, 0:1] == occ_lane, occ[...], 0.0), axis=1, keepdims=True)
-    e_j = jnp.sum(jnp.where(rows[:, 1:2] == occ_lane, occ[...], 0.0), axis=1, keepdims=True)
-    den_buf[...] = vir[...] - (e_i + e_j)
+    square = (ROWS, ROWS)
+    diagonal = lax.broadcasted_iota(jnp.int32, square, 0) == lax.broadcasted_iota(jnp.int32, square, 1)
+
+    def energy(which):
+        orbital = jnp.where(diagonal, rows[which : which + 1, :].astype(F32), 0.0)
+        orbital = jnp.sum(orbital, axis=1, keepdims=True).astype(jnp.int32)
+        return jnp.sum(jnp.where(orbital == occ_lane, occ[...], 0.0), axis=1, keepdims=True)
+
+    den_buf[...] = vir[...] - (energy(0) + energy(1))
     acc[...] = jnp.zeros_like(acc)
 
     own_ints.wait()
@@ -216,11 +242,13 @@
             mid = rest.astype(BF16)
             low = (rest - mid.astype(F32)).astype(BF16)
             block = (zl + ZLO - ORDER[o]) % ZLO
-            held = block_of[pl.ds(block, 1), :]
-            goes = jnp.zeros((1, LANES), jnp.int32)
-            for j in range(8):
-                goes = jnp.where(column // 16 == j, held[:, j : j + 1], goes)
-            goes = goes * 16 + column % 16
+            rows_at = lax.broadcasted_iota(jnp.int32, (BLOCKS, LANES), 0)
+            pick = rows_at == block * 8 + lax.broadcasted_iota(jnp.int32, (BLOCKS, LANES), 1) // 16
+            goes = lax.dot_general(
+                block_of[...].astype(F32).astype(BF16), jnp.where(pick, 1.0, 0.0).astype(BF16),
+                (((1,), (0,)), ((), ())), preferred_element_type=F32,
+            )
+            goes = goes.astype(jnp.int32) * 16 + column % 16
             place = lax.broadcasted_iota(jnp.int32, (1024, LANES), 0)
             moves = jnp.where(place == goes, 1.0, 0.0).astype(BF16)
             moved = lax.dot_general(
@@ -274,36 +302,35 @@
 
 
 def per_device(amps, ints, block_of, pair_rows, occ_energy, vir_pair_energy):
-    column = lax.axis_index("pair") * RANGE + lax.broadcasted_iota(jnp.int32, (1, RANGE), 1)
-    weighted = ints * jnp.where(column < NV, 1.0, 2.0).astype(BF16)
-    wide = jnp.pad(weighted, ((0, 0), (0, WIDE - RANGE)))
-    tail = jnp.pad(amps[:, TAIL:], ((0, 0), (0, TAIL + PIECE - CD)))
     vmem = pl.BlockSpec(memory_space=pltpu.VMEM)
     hbm = pl.BlockSpec(memory_space=pl.ANY)
     dma = pltpu.SemaphoreType.DMA
     return pl.pallas_call(
         kernel,
         out_shape=jax.ShapeDtypeStruct((ROWS, 1024), F32),
-        in_specs=[hbm, vmem, vmem, vmem, vmem, vmem, vmem],
+        in_specs=[hbm, hbm, vmem, vmem, vmem, vmem],
         out_specs=vmem,
         scratch_shapes=[
             pltpu.VMEM((2, 512, PIECE), BF16),
             pltpu.VMEM((Z, 8, ROWS, PIECE), BF16),
+            pltpu.VMEM((ROWS, RANGE), BF16),
+            pltpu.VMEM((ROWS, CD - TAIL), BF16),
+            pltpu.VMEM((ROWS, PIECE), BF16),
             pltpu.VMEM((ROWS, WIDE), BF16),
             pltpu.VMEM((8, 512, LANES), F32),
             pltpu.VMEM((8, 256, LANES), F32),
             pltpu.VMEM((8, 256, LANES), F32),
             pltpu.VMEM((ROWS, 1024), F32),
             pltpu.VMEM((ROWS, 1024), F32),
-            dma, dma, dma, dma, dma, dma((2,)),
+            dma((2,)), dma, dma, dma, dma, dma, dma((2,)),
             dma((Z, 2)), dma((Z, 2)), dma((5,)), dma((5,)), dma((5,)), dma((5,)),
         ],
         compiler_params=pltpu.CompilerParams(
-            collective_id=0, has_side_effects=True, vmem_limit_bytes=40 * 1024 * 1024
+            collective_id=0, has_side_effects=True, vmem_limit_bytes=56 * 1024 * 1024
         ),
         cost_estimate=pl.CostEstimate(flops=2700000000, bytes_accessed=4000000, transcendentals=0),
     )(
-        amps, tail, wide, block_of.reshape(8, 8), pair_rows,
+        amps, ints, block_of.reshape(1, -1), pair_rows.T,
         occ_energy.reshape(1, -1), vir_pair_energy.reshape(1, -1),
     )
 

time: 95.4 us -> 90.4 us (0.948)
  local copies, waits for them, and re-layouts: 6.01 us -> 1.47 us
  other arithmetic: 1.04 us -> 0 us
    unnamed x8 -> x1, local copies, waits for them, and re-layouts: 4.46 us -> 1.47 us
    mul x1 -> x0, other arithmetic: 1.03 us -> none  [per_device(): weighted = ints * jnp.where(column < NV, 1.0, 2.0).astype(BF16)]
where the time goes in v2:
time: 90.4 us; the launch traced here: 90.2 us
  Pallas kernels  88.7 us (98%)
  local copies, waits for them, and re-layouts  1.47 us (2%)
    pallas_call x1, Pallas kernels, per_device(): pl.pallas_call(kernel, out_shape=jax.ShapeDtypeStruct((ROWS, 1024), F32),...  88.7 us

profile of v2, /device:TPU:1, one launch (start us, length us, event | category | flops | bytes accessed | tf_op | source)
XLA Modules:
  0.0 90.2 jit_solution(6590256478109503217)
XLA Ops:
  0.0 88.7 %shard_map.64 = f32[16,1024]{1,0:T(8,128)} custom-call(bf16[16,80200]{1,0:T(8,128)(2,1)} %amps.1, bf16[16,10025]{1,0:T(8,128)(2,1)} %ints.1, s32[1,64]{1,0:T(1,128)} %bitcast.6, s32[2,16]{1,0:T(2,128)} %bitcast.5, f32[1,120]{1,0:T(1,128)} %bitcast.7, f32[1,1024]{1,0:T(1,128)} %bitcast.4), custom_call_target="tpu_custom_call" | custom-call | flops 2700000000 | bytes 4000000 | tf_op jit(solution)/shard_map/pallas_call | solution.py:308
  88.7 1.5 %copy.8 = f32[16,1024]{1,0:T(8,128)} copy(f32[16,1024]{1,0:T(8,128)} %shard_map.64) | data formatting | bytes 131072

commit v3 on v1

v3 whole, which is shorter than its diff:
```python
import functools

import jax
import jax.numpy as jnp
from jax import lax
from jax.experimental import pallas as pl
from jax.experimental.pallas import tpu as pltpu
from jax.sharding import PartitionSpec as P

NV = 400
CD = 80200
RANGE = 10025
LANES = 128
WIDE = 10240
PIECE = 1280
LAST_TILE = 547
TAIL = LAST_TILE * LANES + WIDE - PIECE
Z, ZLO, Y, X = 16, 8, 4, 4
PLANE = 32
BLOCKS = 64
ROWS = 16
MESH = pl.DeviceIdType.MESH
F32, BF16 = jnp.float32, jnp.bfloat16

ORDER = (4, 3, 5, 2, 6, 1, 7, 0)
GROUPS = ((0, 1), (1, 3), (3, 5), (5, 7), (7, 8))
FIRST = (0, 1, 2, 3, 4, 5, 14, 15)
NEAR = (0, 1, 3, 2)
NT = (((1,), (1,)), ((), ()))


def first_tile(p):
    return jnp.minimum(lax.div(RANGE * p, LANES), LAST_TILE)


def kernel(
    amps, ints, block_of, rows, occ, vir, out,
    a_buf, g_buf, held, last, tail, prep, part, sib, got, acc, den_buf, in_sem,
    i_send, i_recv, i_own, a_send, a_recv, a_own, r_send, r_recv, s_send, s_recv, q_send, q_recv,
):
    pair, blk = lax.axis_index("pair"), lax.axis_index("blk")
    zh, y = lax.div(pair, Y), lax.rem(pair, Y)
    zl, x, c = lax.div(blk, X * 2), lax.rem(lax.div(blk, 2), X), lax.rem(blk, 2)
    z = zh * ZLO + zl

    def plane(z_at):
        return lax.div(z_at, ZLO) * Y, lax.rem(z_at, ZLO) * (X * 2)

    row, column = plane(z)
    ys, xs = [lax.rem(y + d, Y) for d in range(Y)], [lax.rem(x + d, X) for d in range(X)]
    up, down = plane(lax.rem(z + 1, Z)), plane(lax.rem(z + Z - 1, Z))
    up, down = ((p + y, b + x * 2 + c) for p, b in (up, down))
    twin = (pair, column + x * 2 + 1 - c)

    def device(y_at, x_at, c_at):
        return (row + y_at, column + x_at * 2 + c_at)

    def peer(k):
        dc, dy, dx = lax.div(k, 16), lax.rem(lax.div(k, 4), 4), lax.rem(k, 4)
        return lax.rem(y + dy, Y), lax.rem(x + dx, X), lax.rem(c + dc, 2)

    get_ints = pltpu.make_async_copy(ints, held, in_sem.at[0])
    get_ints.start()
    get_tail = pltpu.make_async_copy(amps.at[:, TAIL:CD], last.at[:, :], in_sem.at[1])
    get_tail.start()

    barrier = pltpu.get_barrier_semaphore()

    def greet(k, carry):
        pl.semaphore_signal(barrier, inc=1, device_id=device(*peer(k)), device_id_type=MESH)
        return carry

    lax.fori_loop(1, PLANE, greet, 0)
    for where in (up, down):
        pl.semaphore_signal(barrier, inc=1, device_id=where, device_id_type=MESH)

    offset = RANGE * pair - first_tile(pair) * LANES
    shift, skip = lax.rem(offset, LANES), lax.div(offset, LANES)
    lane = lax.broadcasted_iota(jnp.int32, (ROWS, LANES), 1)
    keep = lane >= shift

    def put(tile, value, before):
        now = pltpu.roll(value, shift, 1)
        to = pl.multiple_of(lax.rem(tile + skip, 80) * LANES, LANES)
        prep[:, pl.ds(to, LANES)] = jnp.where(keep, now, before).astype(BF16)
        return now

    def align(i, before):
        for j in range(6):
            tile = i * 6 + j
            at = pl.ds(pl.multiple_of(tile * LANES, LANES), LANES)
            column = RANGE * pair + tile * LANES + lane
            weight = jnp.where(column < NV, 1.0, 2.0)
            before = put(tile, held[:, at].astype(F32) * weight, before)
        return before

    get_ints.wait()
    before = lax.fori_loop(0, 13, align, jnp.zeros((ROWS, LANES), F32))
    rest = held[:, 78 * LANES : RANGE].astype(F32) * 2.0
    rest = jnp.concatenate([rest, jnp.zeros((ROWS, 79 * LANES - RANGE), F32)], axis=1)
    before = put(78, rest, before)
    put(79, jnp.zeros((ROWS, LANES), F32), before)
    get_tail.wait()
    tail[:, 0 : PIECE - LANES] = last[:, 0 : PIECE - LANES]
    ending = last[:, PIECE - LANES :]
    tail[:, PIECE - LANES :] = jnp.concatenate([ending, jnp.zeros((ROWS, TAIL + PIECE - CD), BF16)], axis=1)

    pl.semaphore_wait(barrier, PLANE - 1 + 2)

    def ints_copy(x_to, c_to):
        src = prep.at[:, pl.ds(pl.multiple_of((x_to * 2 + c_to) * PIECE, LANES), PIECE)]
        return src, g_buf.at[0, x * 2 + c]

    def send_ints(e, x_to, c_to):
        src, dst = ints_copy(x_to, c_to)
        pltpu.make_async_remote_copy(
            src, dst, i_send, i_recv.at[e], device_id=device(y, x_to, c_to), device_id_type=MESH
        ).start()

    send_ints(0, x, 1 - c)

    def amps_at(half, y_to, x_to, c_to):
        q = x_to * 2 + c_to
        p = half * Y + y_to
        start = pl.multiple_of(first_tile(p) * LANES + q * PIECE, LANES)
        return start, jnp.logical_and(p == 7, q == 7)

    def send_amps(k, carry):
        y_to, x_to, c_to = peer(k)
        for half in range(2):
            start, ends = amps_at(half, y_to, x_to, c_to)
            dst = a_buf.at[half, pl.ds(pl.multiple_of(k * ROWS, ROWS), ROWS)]

            @pl.when(jnp.logical_not(ends))
            def _():
                pltpu.make_async_remote_copy(
                    amps.at[:, pl.ds(start, PIECE)], dst, a_send, a_recv,
                    device_id=device(y_to, x_to, c_to), device_id_type=MESH,
                ).start()

            @pl.when(ends)
            def _():
                pltpu.make_async_remote_copy(
                    tail, dst, a_send, a_recv,
                    device_id=device(y_to, x_to, c_to), device_id_type=MESH,
                ).start()

        return carry

    for half in range(2):
        start, ends = amps_at(half, y, x, c)
        dst = a_buf.at[half, 0:ROWS]

        @pl.when(jnp.logical_not(ends))
        def _():
            pltpu.make_async_copy(amps.at[:, pl.ds(start, PIECE)], dst, a_own.at[half]).start()

        @pl.when(ends)
        def _():
            pltpu.make_async_copy(tail, dst, a_own.at[half]).start()

    def hop(m_from, m_to, at, where):
        sl = pl.ds(xs[-NEAR[at] % X] * 2, 2)
        return pltpu.make_async_remote_copy(
            g_buf.at[m_from, sl], g_buf.at[m_to, sl], r_send, r_recv.at[m_to, at],
            device_id=where, device_id_type=MESH,
        )

    def forward(step, quarters=range(4)):
        for at in quarters:
            ways = [(step, (step - 1) % Z, up), (Z - step, (Z - step + 1) % Z, down)]
            if step == 8:
                ways = [ways[at // 2]]
            if step == 1 and at == 0:
                continue
            if step == 1:
                came = g_buf.at[0, 0:2]
                pltpu.make_async_copy(came, came, i_recv.at[NEAR[at]]).wait()
            for m_to, m_from, where in ways:
                if step > 1:
                    hop(m_from, m_from, at, where).wait_recv()
                hop(m_from, m_to, at, where).start()
            if step == 1:
                lax.fori_loop(at * 8, at * 8 + 8, send_amps, 0)

    def start_ring():
        mine = pltpu.make_async_copy(*ints_copy(x, c), i_own)
        came = g_buf.at[0, 0]
        for own in (True, False):
            at = x * 2 + c if own else x * 2 + 1 - c
            if not own:
                pltpu.make_async_copy(came, came, i_recv.at[0]).wait()
            for m_to, where in ((1, up), (Z - 1, down)):
                pltpu.make_async_remote_copy(
                    ints_copy(x, c)[0] if own else g_buf.at[0, at], g_buf.at[m_to, at],
                    r_send, r_recv.at[m_to, 0], device_id=where, device_id_type=MESH,
                ).start()
            if own:
                mine.start()
                for e in NEAR[1:]:
                    for c_to in (c, 1 - c):
                        send_ints(e, xs[e], c_to)
        lax.fori_loop(1, 8, send_amps, 0)
        return mine

    def multiply(*slots, lines=slice(0, 512)):
        for m in slots:
            o = ORDER.index(m % 8)
            half = lax.div(lax.rem(z + Z - m, Z), ZLO)
            product = lax.dot_general(
                a_buf[half, lines], g_buf[m].reshape(LANES, PIECE), NT, preferred_element_type=F32
            )
            part[o, lines] = product if m in FIRST else part[o, lines] + product

    def twin_copy(group):
        lo, hi = GROUPS[group]
        return pltpu.make_async_remote_copy(
            part.at[lo:hi, 256:512], sib.at[lo:hi], s_send, s_recv.at[group],
            device_id=twin, device_id_type=MESH,
        )

    def spread(group):
        lo, hi = GROUPS[group]
        twin_copy(group).wait_recv()
        for o in range(lo, hi):
            part[o, 0:256] += sib[o]

        for k in range(1, 16):
            sl = slice(k * ROWS, (k + 1) * ROWS)
            pltpu.make_async_remote_copy(
                part.at[lo:hi, sl], got.at[lo:hi, sl], q_send, q_recv.at[group],
                device_id=device(ys[-(k // 4) % Y], xs[-k % X], c), device_id_type=MESH,
            ).start()

    def finish(group):
        lo, hi = GROUPS[group]
        arrived = got.at[lo:hi, ROWS:256]
        pltpu.make_async_copy(arrived, arrived, q_recv.at[group]).wait()
        spot = lax.broadcasted_iota(jnp.int32, (1, LANES), 1)
        for o in range(lo, hi):
            total = part[o, 0:ROWS]
            for k in range(1, 16):
                total = total + got[o, k * ROWS : (k + 1) * ROWS]
            top = total.astype(BF16)
            rest = total - top.astype(F32)
            mid = rest.astype(BF16)
            low = (rest - mid.astype(F32)).astype(BF16)
            block = lax.rem(zl + ZLO - ORDER[o], ZLO)
            rows_at = lax.broadcasted_iota(jnp.int32, (BLOCKS, LANES), 0)
            pick = rows_at == block * 8 + lax.broadcasted_iota(jnp.int32, (BLOCKS, LANES), 1) // 16
            goes = lax.dot_general(
                block_of[...].astype(F32).astype(BF16), jnp.where(pick, 1.0, 0.0).astype(BF16),
                (((1,), (0,)), ((), ())), preferred_element_type=F32,
            )
            goes = goes.astype(jnp.int32) * 16 + spot % 16
            place = lax.broadcasted_iota(jnp.int32, (1024, LANES), 0)
            moves = jnp.where(place == goes, 1.0, 0.0).astype(BF16)
            moved = lax.dot_general(
                jnp.concatenate([top, mid, low], axis=0), moves, NT, preferred_element_type=F32
            )
            acc[...] += moved[0:16] + moved[16:32] + moved[32:48]

    own_ints = start_ring()
    forward(1)
    occ_lane = lax.broadcasted_iota(jnp.int32, (ROWS, occ.shape[1]), 1)
    square = (ROWS, ROWS)
    diagonal = lax.broadcasted_iota(jnp.int32, square, 0) == lax.broadcasted_iota(jnp.int32, square, 1)

    def energy(which):
        orbital = jnp.where(diagonal, rows[which : which + 1, :].astype(F32), 0.0)
        orbital = jnp.sum(orbital, axis=1, keepdims=True).astype(jnp.int32)
        return jnp.sum(jnp.where(orbital == occ_lane, occ[...], 0.0), axis=1, keepdims=True)

    den_buf[...] = vir[...] - (energy(0) + energy(1))
    acc[...] = jnp.zeros_like(acc)

    for step in range(2, 7):
        forward(step)
    pltpu.make_async_copy(amps.at[:, 0:PIECE], a_buf.at[0, 0:ROWS], a_own.at[0]).wait()
    pltpu.make_async_copy(amps.at[:, 0:PIECE], a_buf.at[1, 0:ROWS], a_own.at[1]).wait()
    others = a_buf.at[:, ROWS:512]
    pltpu.make_async_copy(others, others, a_recv).wait()
    own_ints.wait()
    multiply(4, 12)
    twin_copy(0).start()
    forward(7, (0,))
    multiply(3, 11)
    spread(0)
    forward(7, (1,))
    multiply(5, 13)
    twin_copy(1).start()
    forward(7, (2,))
    multiply(2, 14)
    spread(1)
    forward(7, (3,))
    multiply(10, 6)
    twin_copy(2).start()
    forward(8, (0,))
    multiply(1)
    spread(2)
    forward(8, (1,))
    multiply(15)
    finish(0)
    forward(8, (2,))
    multiply(0)
    finish(1)
    forward(8, (3,))
    for at in range(4):
        if at < 2:
            hop(9, 9, at, down).wait_recv()
        else:
            hop(7, 7, at, up).wait_recv()
    multiply(9, 7, lines=slice(256, 512))
    twin_copy(3).start()
    multiply(9, 7, lines=slice(0, 256))
    spread(3)
    finish(2)
    for at in range(4):
        hop(8, 8, at, up).wait_recv()
    multiply(8, lines=slice(256, 512))
    twin_copy(4).start()
    multiply(8, lines=slice(0, 256))
    spread(4)
    finish(3)
    finish(4)
    out[...] = acc[...] / den_buf[...]

    seven = g_buf.at[0, 0:7]
    pltpu.make_async_copy(seven, seven, i_send).wait()
    pltpu.make_async_copy(others, others, a_send).wait()
    for whole, sem in [(g_buf.at[1:Z], r_send), (sib, s_send), (got.at[:, ROWS:256], q_send)]:
        pltpu.make_async_copy(whole, whole, sem).wait()


def per_device(amps, ints, block_of, pair_rows, occ_energy, vir_pair_energy):
    vmem = pl.BlockSpec(memory_space=pltpu.VMEM)
    hbm = pl.BlockSpec(memory_space=pltpu.HBM)
    dma = pltpu.SemaphoreType.DMA
    return pl.pallas_call(
        kernel,
        out_shape=jax.ShapeDtypeStruct((ROWS, 1024), F32),
        in_specs=[hbm, hbm, vmem, vmem, vmem, vmem],
        out_specs=vmem,
        scratch_shapes=[
            pltpu.VMEM((2, 512, PIECE), BF16),
            pltpu.VMEM((Z, 8, ROWS, PIECE), BF16),
            pltpu.VMEM((ROWS, RANGE), BF16),
            pltpu.VMEM((ROWS, CD - TAIL), BF16),
            pltpu.VMEM((ROWS, PIECE), BF16),
            pltpu.VMEM((ROWS, WIDE), BF16),
            pltpu.VMEM((8, 512, LANES), F32),
            pltpu.VMEM((8, 256, LANES), F32),
            pltpu.VMEM((8, 256, LANES), F32),
            pltpu.VMEM((ROWS, 1024), F32),
            pltpu.VMEM((ROWS, 1024), F32),
            dma((2,)), dma, dma((4,)), dma, dma, dma, dma((2,)),
            dma, dma((Z, 4)), dma, dma((5,)), dma, dma((5,)),
        ],
        compiler_params=pltpu.CompilerParams(
            collective_id=0, has_side_effects=True, vmem_limit_bytes=56 * 1024 * 1024
        ),
        cost_estimate=pl.CostEstimate(flops=2700000000, bytes_accessed=4000000, transcendentals=0),
    )(
        amps, ints, block_of.reshape(1, -1), pair_rows.T,
        occ_energy.reshape(1, -1), vir_pair_energy.reshape(1, -1),
    )


def solution(mesh):
    placed = (P(("blk", "pair"), None), P("blk", "pair"), P(), P(("blk", "pair"), None), P(), P())
    return jax.shard_map(
        per_device, mesh=mesh, in_specs=placed, out_specs=P(("blk", "pair"), None), check_vma=False
    )
```

time: 95.4 us -> 84.9 us (0.89)
  Pallas kernels: 88.1 us -> 83.2 us
  local copies, waits for them, and re-layouts: 6.01 us -> 1.47 us
  other arithmetic: 1.04 us -> 0 us
    pallas_call x1, Pallas kernels: 88.1 us -> 83.2 us  [per_device(): pl.pallas_call(kernel, out_shape=jax.ShapeDtypeStruct((ROWS, 1024), F32),...]
    unnamed x8 -> x1, local copies, waits for them, and re-layouts: 4.46 us -> 1.47 us
    mul x1 -> x0, other arithmetic: 1.03 us -> none  [per_device(): weighted = ints * jnp.where(column < NV, 1.0, 2.0).astype(BF16)]
where the time goes in v3:
time: 84.9 us; the launch traced here: 84.7 us
  Pallas kernels  83.2 us (98%)
  local copies, waits for them, and re-layouts  1.47 us (2%)
    pallas_call x1, Pallas kernels, per_device(): pl.pallas_call(kernel, out_shape=jax.ShapeDtypeStruct((ROWS, 1024), F32),...  83.2 us

profile of v3, /device:TPU:1, one launch (start us, length us, event | category | flops | bytes accessed | tf_op | source)
XLA Modules:
  0.0 84.7 jit_solution(15326523487056257599)
XLA Ops:
  0.0 83.2 %shard_map.64 = f32[16,1024]{1,0:T(8,128)} custom-call(bf16[16,80200]{1,0:T(8,128)(2,1)} %amps.1, bf16[16,10025]{1,0:T(8,128)(2,1)} %ints.1, s32[1,64]{1,0:T(1,128)} %bitcast.6, s32[2,16]{1,0:T(2,128)} %bitcast.5, f32[1,120]{1,0:T(1,128)} %bitcast.7, f32[1,1024]{1,0:T(1,128)} %bitcast.4), custom_call_target="tpu_custom_call" | custom-call | flops 2700000000 | bytes 4000000 | tf_op jit(solution)/shard_map/pallas_call | solution.py:339
  83.2 1.5 %copy.8 = f32[16,1024]{1,0:T(8,128)} copy(f32[16,1024]{1,0:T(8,128)} %shard_map.64) | data formatting | bytes 131072

commit v4 on v3

--- a/solution.py
+++ b/solution.py
@@ -7,6 +7,7 @@
 from jax.experimental.pallas import tpu as pltpu
 from jax.sharding import PartitionSpec as P
 
+NO = 120
 NV = 400
 CD = 80200
 RANGE = 10025
@@ -25,6 +26,7 @@
 ORDER = (4, 3, 5, 2, 6, 1, 7, 0)
 GROUPS = ((0, 1), (1, 3), (3, 5), (5, 7), (7, 8))
 FIRST = (0, 1, 2, 3, 4, 5, 14, 15)
+FAR = (10, 6, 14, 9, 11, 2, 8, 5, 7, 13, 15, 1, 3, 4, 12)
 NEAR = (0, 1, 3, 2)
 NT = (((1,), (1,)), ((), ()))
 
@@ -34,9 +36,16 @@
 
 
 def kernel(
-    amps, ints, block_of, rows, occ, vir, out,
+    amps, ints, *rest,
+):
+    small, (out, *scratch) = rest[:4], rest[4:]
+    run(amps, ints, small, out, *scratch)
+
+
+def run(
+    amps, ints, small, out, block_of, rows, occ, vir, small_sem,
     a_buf, g_buf, held, last, tail, prep, part, sib, got, acc, den_buf, in_sem,
-    i_send, i_recv, i_own, a_send, a_recv, a_own, r_send, r_recv, s_send, s_recv, q_send, q_recv,
+    i_send, i_recv, i_own, a_send, a_recv, a_own, r_send, r_recv, f_send, s_send, s_recv, q_send, q_recv,
 ):
     pair, blk = lax.axis_index("pair"), lax.axis_index("blk")
     zh, y = lax.div(pair, Y), lax.rem(pair, Y)
@@ -64,15 +73,20 @@
     get_tail = pltpu.make_async_copy(amps.at[:, TAIL:CD], last.at[:, :], in_sem.at[1])
     get_tail.start()
 
+    get_small = [
+        pltpu.make_async_copy(src, dst, small_sem.at[i])
+        for i, (src, dst) in enumerate(zip(small, (block_of, rows, occ, vir)))
+    ]
+
     barrier = pltpu.get_barrier_semaphore()
 
     def greet(k, carry):
         pl.semaphore_signal(barrier, inc=1, device_id=device(*peer(k)), device_id_type=MESH)
         return carry
 
-    lax.fori_loop(1, PLANE, greet, 0)
     for where in (up, down):
         pl.semaphore_signal(barrier, inc=1, device_id=where, device_id_type=MESH)
+    lax.fori_loop(1, PLANE, greet, 0)
 
     offset = RANGE * pair - first_tile(pair) * LANES
     shift, skip = lax.rem(offset, LANES), lax.div(offset, LANES)
@@ -94,6 +108,8 @@
             before = put(tile, held[:, at].astype(F32) * weight, before)
         return before
 
+    for copy in get_small:
+        copy.start()
     get_ints.wait()
     before = lax.fori_loop(0, 13, align, jnp.zeros((ROWS, LANES), F32))
     rest = held[:, 78 * LANES : RANGE].astype(F32) * 2.0
@@ -166,11 +182,23 @@
             device_id=where, device_id_type=MESH,
         )
 
+    def from_below(z_at):
+        return jnp.minimum(lax.div(z_at + 1, 2), 2)
+
+    def last_hops(at):
+        sl = pl.ds(xs[-NEAR[at] % X] * 2, 2)
+        for side, (m_from, where, wanted) in enumerate((
+            (7, up, at < from_below(lax.rem(z + 1, Z))),
+            (9, down, at >= from_below(lax.rem(z + Z - 1, Z))),
+        )):
+            yield wanted, pltpu.make_async_remote_copy(
+                g_buf.at[m_from, sl], g_buf.at[8, sl], f_send.at[at, side], r_recv.at[8, at],
+                device_id=where, device_id_type=MESH,
+            )
+
     def forward(step, quarters=range(4)):
         for at in quarters:
             ways = [(step, (step - 1) % Z, up), (Z - step, (Z - step + 1) % Z, down)]
-            if step == 8:
-                ways = [ways[at // 2]]
             if step == 1 and at == 0:
                 continue
             if step == 1:
@@ -179,9 +207,11 @@
             for m_to, m_from, where in ways:
                 if step > 1:
                     hop(m_from, m_from, at, where).wait_recv()
-                hop(m_from, m_to, at, where).start()
-            if step == 1:
-                lax.fori_loop(at * 8, at * 8 + 8, send_amps, 0)
+                if step < 8:
+                    hop(m_from, m_to, at, where).start()
+            if step == 8:
+                for wanted, copy in last_hops(at):
+                    pl.when(wanted)(copy.start)
 
     def start_ring():
         mine = pltpu.make_async_copy(*ints_copy(x, c), i_own)
@@ -200,7 +230,6 @@
                 for e in NEAR[1:]:
                     for c_to in (c, 1 - c):
                         send_ints(e, xs[e], c_to)
-        lax.fori_loop(1, 8, send_amps, 0)
         return mine
 
     def multiply(*slots, lines=slice(0, 512)):
@@ -225,7 +254,7 @@
         for o in range(lo, hi):
             part[o, 0:256] += sib[o]
 
-        for k in range(1, 16):
+        for k in FAR:
             sl = slice(k * ROWS, (k + 1) * ROWS)
             pltpu.make_async_remote_copy(
                 part.at[lo:hi, sl], got.at[lo:hi, sl], q_send, q_recv.at[group],
@@ -262,6 +291,9 @@
 
     own_ints = start_ring()
     forward(1)
+    lax.fori_loop(1, PLANE, send_amps, 0)
+    for copy in get_small:
+        copy.wait()
     occ_lane = lax.broadcasted_iota(jnp.int32, (ROWS, occ.shape[1]), 1)
     square = (ROWS, ROWS)
     diagonal = lax.broadcasted_iota(jnp.int32, square, 0) == lax.broadcasted_iota(jnp.int32, square, 1)
@@ -305,11 +337,6 @@
     multiply(0)
     finish(1)
     forward(8, (3,))
-    for at in range(4):
-        if at < 2:
-            hop(9, 9, at, down).wait_recv()
-        else:
-            hop(7, 7, at, up).wait_recv()
     multiply(9, 7, lines=slice(256, 512))
     twin_copy(3).start()
     multiply(9, 7, lines=slice(0, 256))
@@ -328,8 +355,11 @@
     seven = g_buf.at[0, 0:7]
     pltpu.make_async_copy(seven, seven, i_send).wait()
     pltpu.make_async_copy(others, others, a_send).wait()
-    for whole, sem in [(g_buf.at[1:Z], r_send), (sib, s_send), (got.at[:, ROWS:256], q_send)]:
+    for whole, sem in [(g_buf.at[0 : Z - 2], r_send), (sib, s_send), (got.at[:, ROWS:256], q_send)]:
         pltpu.make_async_copy(whole, whole, sem).wait()
+    for at in range(4):
+        for wanted, copy in last_hops(at):
+            pl.when(wanted)(copy.wait_send)
 
 
 def per_device(amps, ints, block_of, pair_rows, occ_energy, vir_pair_energy):
@@ -339,9 +369,11 @@
     return pl.pallas_call(
         kernel,
         out_shape=jax.ShapeDtypeStruct((ROWS, 1024), F32),
-        in_specs=[hbm, hbm, vmem, vmem, vmem, vmem],
+        in_specs=[hbm] * 6,
         out_specs=vmem,
         scratch_shapes=[
+            pltpu.VMEM((1, BLOCKS), jnp.int32), pltpu.VMEM((2, ROWS), jnp.int32),
+            pltpu.VMEM((1, NO), F32), pltpu.VMEM((1, 1024), F32), dma((4,)),
             pltpu.VMEM((2, 512, PIECE), BF16),
             pltpu.VMEM((Z, 8, ROWS, PIECE), BF16),
             pltpu.VMEM((ROWS, RANGE), BF16),
@@ -354,7 +386,7 @@
             pltpu.VMEM((ROWS, 1024), F32),
             pltpu.VMEM((ROWS, 1024), F32),
             dma((2,)), dma, dma((4,)), dma, dma, dma, dma((2,)),
-            dma, dma((Z, 4)), dma, dma((5,)), dma, dma((5,)),
+            dma, dma((Z, 4)), dma((4, 2)), dma, dma((5,)), dma, dma((5,)),
         ],
         compiler_params=pltpu.CompilerParams(
             collective_id=0, has_side_effects=True, vmem_limit_bytes=56 * 1024 * 1024

time: 84.9 us -> 82 us (0.966)
  Pallas kernels: 83.2 us -> 80.3 us
    pallas_call x1, Pallas kernels: 83.2 us -> 80.3 us  [per_device(): pl.pallas_call(kernel, out_shape=jax.ShapeDtypeStruct((ROWS, 1024), F32),...]
where the time goes in v4:
time: 82 us; the launch traced here: 81.8 us
  Pallas kernels  80.3 us (98%)
  local copies, waits for them, and re-layouts  1.47 us (2%)
    pallas_call x1, Pallas kernels, per_device(): pl.pallas_call(kernel, out_shape=jax.ShapeDtypeStruct((ROWS, 1024), F32),...  80.3 us

profile of v4, /device:TPU:1, one launch (start us, length us, event | category | flops | bytes accessed | tf_op | source)
XLA Modules:
  0.0 81.8 jit_solution(10241056466203828559)
XLA Ops:
  0.0 80.3 %shard_map.64 = f32[16,1024]{1,0:T(8,128)} custom-call(bf16[16,80200]{1,0:T(8,128)(2,1)} %amps.1, bf16[16,10025]{1,0:T(8,128)(2,1)} %ints.1, s32[1,64]{1,0:T(1,128)} %bitcast.6, s32[2,16]{1,0:T(2,128)} %bitcast.5, f32[1,120]{1,0:T(1,128)} %bitcast.7, f32[1,1024]{1,0:T(1,128)} %bitcast.4), custom_call_target="tpu_custom_call" | custom-call | flops 2700000000 | bytes 4000000 | tf_op jit(solution)/shard_map/pallas_call | solution.py:369
  80.3 1.5 %copy.8 = f32[16,1024]{1,0:T(8,128)} copy(f32[16,1024]{1,0:T(8,128)} %shard_map.64) | data formatting | bytes 131072

commit v5 on v4

--- a/solution.py
+++ b/solution.py
@@ -183,7 +183,7 @@
         )
 
     def from_below(z_at):
-        return jnp.minimum(lax.div(z_at + 1, 2), 2)
+        return jnp.minimum(lax.div(z_at, 2), 2)
 
     def last_hops(at):
         sl = pl.ds(xs[-NEAR[at] % X] * 2, 2)
@@ -290,8 +290,9 @@
             acc[...] += moved[0:16] + moved[16:32] + moved[32:48]
 
     own_ints = start_ring()
-    forward(1)
+    forward(1, (0, 1, 2))
     lax.fori_loop(1, PLANE, send_amps, 0)
+    forward(1, (3,))
     for copy in get_small:
         copy.wait()
     occ_lane = lax.broadcasted_iota(jnp.int32, (ROWS, occ.shape[1]), 1)

time: 82 us -> 82.2 us (level)
  no operation moved by 1% of the time
where the time goes in v5:
time: 82.2 us; the launch traced here: 82.1 us
  Pallas kernels  80.6 us (98%)
  local copies, waits for them, and re-layouts  1.47 us (2%)
    pallas_call x1, Pallas kernels, per_device(): pl.pallas_call(kernel, out_shape=jax.ShapeDtypeStruct((ROWS, 1024), F32),...  80.6 us

profile of v5, /device:TPU:1, one launch (start us, length us, event | category | flops | bytes accessed | tf_op | source)
XLA Modules:
  0.0 82.1 jit_solution(4738751198733793662)
XLA Ops:
  0.0 80.6 %shard_map.64 = f32[16,1024]{1,0:T(8,128)} custom-call(bf16[16,80200]{1,0:T(8,128)(2,1)} %amps.1, bf16[16,10025]{1,0:T(8,128)(2,1)} %ints.1, s32[1,64]{1,0:T(1,128)} %bitcast.6, s32[2,16]{1,0:T(2,128)} %bitcast.5, f32[1,120]{1,0:T(1,128)} %bitcast.7, f32[1,1024]{1,0:T(1,128)} %bitcast.4), custom_call_target="tpu_custom_call" | custom-call | flops 2700000000 | bytes 4000000 | tf_op jit(solution)/shard_map/pallas_call | solution.py:370
  80.6 1.5 %copy.8 = f32[16,1024]{1,0:T(8,128)} copy(f32[16,1024]{1,0:T(8,128)} %shard_map.64) | data formatting | bytes 131072
